TPU v7x, 32 devices: a whole 2x2x4 slice. The times are simulated.
32 devices in a mesh: groups: 2 (over y), ctx: 16 (over z, x, core).
Axes of the slice: x: 2, y: 2, z: 4, core: 2. Of those that a mesh axis runs over, the one named last changes fastest.
Arguments:
- queries: bfloat16 [4096, 4096], P(('groups', 'ctx')), parts along dimension 0, may hold values from -6 to 6
- keys: bfloat16 [4096, 512], P(('groups', 'ctx')), parts along dimension 0, may hold values from -6 to 6
- values: bfloat16 [4096, 512], P(('groups', 'ctx')), parts along dimension 0, may hold values from -6 to 6
- out_grad: bfloat16 [4096, 4096], P(('groups', 'ctx')), parts along dimension 0, may hold values from -6 to 6
- attn_out: bfloat16 [4096, 4096], P(('groups', 'ctx')), parts along dimension 0, may hold values from -6 to 6
- doc_ids: int32 [4096], P(('groups', 'ctx')), parts along dimension 0, may hold values from 0 to 3, never falling along the last dimension, each value on 1 to 1024 neighbouring positions
Outputs:
- query_grad: bfloat16 [4096, 4096], P(('groups', 'ctx')), parts along dimension 0
- key_grad: bfloat16 [4096, 512], P(('groups', 'ctx')), parts along dimension 0
- value_gradient: bfloat16 [4096, 512], P(('groups', 'ctx')), parts along dimension 0
There are 2 independent parts, one for each index of `groups`. A program takes and returns all parts, laid end to end along the dimension named above; each array names one. Nothing has to cross between parts.
Inputs may be any that keep to these rules, and one draw needn't show every extreme that they name: `doc_ids`: ids never fall along the sequence; every document has at most 1024 tokens and one has exactly 1024.
All inputs are finite; a program needn't handle non-finite values.
Results may differ from a plain program's by a relative error of at most 0.0055.
Values may be sent and summed in bfloat16 or wider, within the bound.
A program may use at most 128 MiB of HBM per device.

v0:
```python
import math

import jax
import jax.numpy as jnp
from jax import lax
from jax.sharding import PartitionSpec as P

HEAD_DIM = 128
HEADS = 32
KV_HEADS = 4
REACH = 8


def attend(
    query_tile, gradient_tile, delta_blk, key_window_slice, value_window_slice, visible, score_scale
):
    scores = (
        jnp.einsum("its,ios->ito", query_tile, key_window_slice, preferred_element_type=jnp.float32)
        * score_scale
    )
    scores = jnp.where(visible, scores, -jnp.inf)
    row_max = jnp.max(scores, axis=2, keepdims=True)
    raw_weights = jnp.where(visible, jnp.exp(scores - row_max), 0.0)
    softmax_w = raw_weights / jnp.sum(raw_weights, axis=2, keepdims=True)
    probability_lowprec = softmax_w.astype(jnp.bfloat16)
    value_gradient = jnp.einsum(
        "zvp,zvh->zph", probability_lowprec, gradient_tile, preferred_element_type=jnp.float32
    )
    probability_gradient = jnp.einsum(
        "its,ios->ito", gradient_tile, value_window_slice, preferred_element_type=jnp.float32
    )
    score_lowprec = (softmax_w * (probability_gradient - delta_blk[:, :, None])).astype(
        jnp.bfloat16
    )
    query_grad = (
        jnp.einsum(
            "ilh,ihj->ilj", score_lowprec, key_window_slice, preferred_element_type=jnp.float32
        )
        * score_scale
    )
    key_grad = (
        jnp.einsum("zvp,zvh->zph", score_lowprec, query_tile, preferred_element_type=jnp.float32)
        * score_scale
    )
    return (query_grad.astype(jnp.bfloat16), key_grad, value_gradient)


def add_block(total, addend, start):
    current = lax.dynamic_slice_in_dim(total, start, addend.shape[0], 0)
    return lax.dynamic_update_slice_in_dim(total, current + addend, start, 0)


def by_heads(
    queries, keys, values, out_grad, attn_out, doc_ids, ranks, my_rank, tok_rows, score_scale
):
    splits = max(1, ranks // HEADS)
    head_units = HEADS * splits
    per_dev = head_units // ranks
    part_rows = tok_rows // splits
    fan_out = ranks // KV_HEADS
    win_len = (REACH + 1) * tok_rows

    def to_units(field):
        field = field.reshape(splits, part_rows, HEADS, HEAD_DIM).transpose(1, 2, 0, 3)
        return field.reshape(part_rows, head_units, HEAD_DIM)

    arrived = lax.all_to_all(
        jnp.stack([to_units(queries), to_units(out_grad), to_units(attn_out)]),
        "ctx",
        split_axis=2,
        concat_axis=1,
        tiled=True,
    )
    delta_got = jnp.sum(arrived[1].astype(jnp.float32) * arrived[2].astype(jnp.float32), axis=2)
    query_all = arrived[0].reshape(ranks, part_rows, per_dev, HEAD_DIM).transpose(2, 0, 1, 3)
    grad_all = arrived[1].reshape(ranks, part_rows, per_dev, HEAD_DIM).transpose(2, 0, 1, 3)
    delta_all = delta_got.reshape(ranks, part_rows, per_dev).transpose(2, 0, 1)
    kv_pair = jnp.stack([keys, values]).reshape(2, tok_rows, KV_HEADS, 1, HEAD_DIM)
    kv_pair = jnp.broadcast_to(kv_pair, (2, tok_rows, KV_HEADS, fan_out, HEAD_DIM)).reshape(
        2, tok_rows, ranks, HEAD_DIM
    )
    kv_full = lax.all_to_all(kv_pair, "ctx", split_axis=2, concat_axis=1, tiled=True)
    lead_zeros = jnp.zeros((2, REACH * tok_rows, HEAD_DIM), kv_full.dtype)
    kv_blocks = jnp.concatenate(
        [lead_zeros, kv_full.reshape(2, ranks * tok_rows, HEAD_DIM)], axis=1
    )
    kv_blocks = kv_blocks.reshape(2, ranks + REACH, tok_rows, HEAD_DIM)
    key_blocks = kv_blocks[0]
    value_blocks = kv_blocks[1]
    doc_full = lax.all_gather(doc_ids, "ctx", axis=0, tiled=True)
    doc_blocks = jnp.concatenate([jnp.zeros((REACH * tok_rows,), jnp.int32), doc_full + 1]).reshape(
        ranks + REACH, tok_rows
    )
    pieces = math.gcd(ranks, max(1, 512 // part_rows))
    groups_q = ranks // pieces
    work_total = per_dev * groups_q
    src_off = jnp.arange(pieces, dtype=jnp.int32)
    win_off = jnp.arange(win_len, dtype=jnp.int32)
    row_off = jnp.arange(part_rows, dtype=jnp.int32)

    def window(blocks, first_src):
        stacked = jnp.stack(
            [
                lax.dynamic_slice_in_dim(blocks, first_src + offset, pieces, 0)
                for offset in range(REACH + 1)
            ],
            axis=1,
        )
        return stacked.reshape((pieces, win_len) + blocks.shape[2:])

    def one_group(totals, work_item):
        key_total, value_total = totals
        unit_no = work_item // groups_q
        first_src = work_item % groups_q * pieces
        zero = jnp.zeros((), jnp.int32)
        part_no = (my_rank * per_dev + unit_no) % splits
        query_tile = lax.dynamic_slice(
            query_all, (unit_no, first_src, zero, zero), (1, pieces, part_rows, HEAD_DIM)
        )[0]
        gradient_tile = lax.dynamic_slice(
            grad_all, (unit_no, first_src, zero, zero), (1, pieces, part_rows, HEAD_DIM)
        )[0]
        delta_blk = lax.dynamic_slice(
            delta_all, (unit_no, first_src, zero), (1, pieces, part_rows)
        )[0]
        key_window_slice = window(key_blocks, first_src)
        value_window_slice = window(value_blocks, first_src)
        doc_win = window(doc_blocks, first_src)
        query_doc = lax.dynamic_slice(
            doc_blocks, (first_src + REACH, part_no * part_rows), (pieces, part_rows)
        )
        src_pos = (first_src + src_off) * tok_rows
        query_pos = src_pos[:, None] + part_no * part_rows + row_off[None, :]
        key_pos = src_pos[:, None] - REACH * tok_rows + win_off[None, :]
        visible = (key_pos[:, None, :] <= query_pos[:, :, None]) & (
            doc_win[:, None, :] == query_doc[:, :, None]
        )
        query_grad, key_grad, value_gradient = attend(
            query_tile,
            gradient_tile,
            delta_blk,
            key_window_slice,
            value_window_slice,
            visible,
            score_scale,
        )
        key_parts = key_grad.reshape(pieces, REACH + 1, tok_rows, HEAD_DIM)
        value_parts = value_gradient.reshape(pieces, REACH + 1, tok_rows, HEAD_DIM)
        for offset in range(REACH + 1):
            key_total = add_block(key_total, key_parts[:, offset], first_src + offset)
            value_total = add_block(value_total, value_parts[:, offset], first_src + offset)
        return ((key_total, value_total), query_grad)

    empty = jnp.zeros((ranks + REACH, tok_rows, HEAD_DIM), jnp.float32)
    totals, query_parts = lax.scan(
        one_group, (empty, empty), jnp.arange(work_total, dtype=jnp.int32)
    )
    query_back = query_parts.reshape(per_dev, ranks, part_rows, HEAD_DIM).transpose(2, 1, 0, 3)
    returned = lax.all_to_all(query_back, "ctx", split_axis=1, concat_axis=2, tiled=True)
    query_grad = (
        returned.reshape(part_rows, HEADS, splits, HEAD_DIM)
        .transpose(2, 0, 1, 3)
        .reshape(tok_rows, HEADS * HEAD_DIM)
    )
    grad_pair = jnp.stack([totals[0][REACH:], totals[1][REACH:]]).reshape(
        2, ranks, 1, tok_rows, HEAD_DIM
    )
    summed = lax.all_to_all(grad_pair, "ctx", split_axis=1, concat_axis=2, tiled=True)
    summed = jnp.sum(summed.reshape(2, KV_HEADS, fan_out, tok_rows, HEAD_DIM), axis=2)
    summed = (
        summed.transpose(0, 2, 1, 3).reshape(2, tok_rows, KV_HEADS * HEAD_DIM).astype(jnp.bfloat16)
    )
    return (query_grad, summed[0], summed[1])


def on_device(queries, keys, values, out_grad, attn_out, doc_ids):
    ranks = lax.axis_size("ctx")
    my_rank = lax.axis_index("ctx")
    tok_rows = queries.shape[0]
    score_scale = 1.0 / math.sqrt(HEAD_DIM)
    return by_heads(
        queries, keys, values, out_grad, attn_out, doc_ids, ranks, my_rank, tok_rows, score_scale
    )


def solution(mesh):
    placed = (
        P(("groups", "ctx"), None),
        P(("groups", "ctx"), None),
        P(("groups", "ctx"), None),
        P(("groups", "ctx"), None),
        P(("groups", "ctx"), None),
        P(("groups", "ctx")),
    )
    return jax.shard_map(
        on_device,
        mesh=mesh,
        in_specs=placed,
        out_specs=(
            P(("groups", "ctx"), None),
            P(("groups", "ctx"), None),
            P(("groups", "ctx"), None),
        ),
        check_vma=False,
    )
```

profile of v0, /device:TPU:0, one launch (start us, length us, event | category | flops | bytes accessed | tf_op | source)
XLA Modules:
  0.0 407.1 jit_solution(13686816865538949824)
XLA Ops:
  4.0 7.5 %all-to-all-start.1 = ((bf16[2,128,16,128]{3,1,0,2:T(8,128)(2,1)}), bf16[2,128,16,128]{3,1,0,2:T(8,128)(2,1)}, u32[]{:S(2)}, u32[]{:S(2)}) async-start(bf16[2,128,16,128]{3,1,0,2:T(8,128)(2,1)} %bitcast.11), calls=%async_computation.1 | async-start | bytes 2097152 | tf_op jit(solution)/shard_map/all_to_all | solution.py:82
  15.5 2.2 pad_maximum_fusion
  17.7 2.0 copy.136
  19.7 14.8 %all-to-all-done.1 = bf16[2,128,16,128]{3,1,0,2:T(8,128)(2,1)} async-done(((bf16[2,128,16,128]{3,1,0,2:T(8,128)(2,1)}), bf16[2,128,16,128]{3,1,0,2:T(8,128)(2,1)}, u32[]{:S(2)}, u32[]{:S(2)}) %all-to-all-start.1) | async-done | bytes 1048608 | tf_op jit(solution)/shard_map/all_to_all | solution.py:82
  34.5 6.9 %all-to-all-start = ((bf16[3,128,32,128]{1,3,0,2:T(8,128)(2,1)}), bf16[3,128,32,128]{1,3,0,2:T(8,128)(2,1)}, u32[]{:S(2)}, u32[]{:S(2)}) async-start(bf16[3,128,32,128]{1,3,0,2:T(8,128)(2,1)} %copy.136), calls=%async_computation | async-start | bytes 6291456 | tf_op jit(solution)/shard_map/all_to_all | solution.py:67
  41.5 67.0 %all-gather = s32[16,1,128]{2,1,0:T(1,128)S(1)} all-gather(s32[1,1,128]{2,1,0:T(1,128)S(1)} %bitcast.446), channel_id=1, replica_groups=mesh['groups'=2,'ctx'=16] {'ctx'}, dimensions={0}, use_global_device_ids=true | all-gather | bytes 8704 | tf_op jit(solution)/shard_map/all_gather | solution.py:90
  111.1 3.5 copy.137
  115.3 1.6 slice_bitcast_fusion.21
  117.2 196.4 %while.18 = (s32[]{:T(128)}, f32[24,128,128]{2,1,0:T(8,128)S(1)}, f32[24,128,128]{2,1,0:T(8,128)S(1)}, bf16[8,4,128,128]{3,2,1,0:T(8,128)(2,1)}, s32[8]{0:T(128)...) while((s32[]{:T(128)}, f32[24,128,128]{2,1,0:T(8,128)S(1)}, ...), condition=%wide.region_4.5_spmd.clone, body=%wide.region_1.4_spmd.clone.sunk | while | flops 766908608 | bytes 68515200 | solution.py:155
  128.9 4.3 %fusion.120 = (f32[4,128]{1,0:T(4,128)S(1)}, f32[4,128,1152]{2,1,0:T(8,128)}) fusion(s32[4,128]{1,0:T(4,128)S(1)} %get-tuple-element.431, s32[4,1152]{1,0:T(4,128)S(1)} %bitcast.432, s32[4,128]{1,0:T(4,128)S(1)} %iota_add_fusion.5, s32[4,1152]{1,0:T(4,128)S(1)} %iota_add_fusion.6, bf16[4,1152,128]{2,1,0:T(8,128)(2,1)} %bitcast.417, ...), kind=kOutput, calls=%fused_computation.136.clone.1 | convolution fusion | flops 157484160 | bytes 3753992 | tf_op jit(solution)/shard_map/while/body/eval_jaxpr/sub | solution.py:23
  133.2 2.7 fusion.122
  137.6 1.6 fusion.121
  153.5 4.2 %fusion.120 = (f32[4,128]{1,0:T(4,128)S(1)}, f32[4,128,1152]{2,1,0:T(8,128)}) fusion(s32[4,128]{1,0:T(4,128)S(1)} %get-tuple-element.431, s32[4,1152]{1,0:T(4,128)S(1)} %bitcast.432, s32[4,128]{1,0:T(4,128)S(1)} %iota_add_fusion.5, s32[4,1152]{1,0:T(4,128)S(1)} %iota_add_fusion.6, bf16[4,1152,128]{2,1,0:T(8,128)(2,1)} %bitcast.417, ...), kind=kOutput, calls=%fused_computation.136.clone.1 | convolution fusion | flops 157484160 | bytes 3753992 | tf_op jit(solution)/shard_map/while/body/eval_jaxpr/sub | solution.py:23
  157.7 2.7 fusion.122
  178.0 4.3 %fusion.120 = (f32[4,128]{1,0:T(4,128)S(1)}, f32[4,128,1152]{2,1,0:T(8,128)}) fusion(s32[4,128]{1,0:T(4,128)S(1)} %get-tuple-element.431, s32[4,1152]{1,0:T(4,128)S(1)} %bitcast.432, s32[4,128]{1,0:T(4,128)S(1)} %iota_add_fusion.5, s32[4,1152]{1,0:T(4,128)S(1)} %iota_add_fusion.6, bf16[4,1152,128]{2,1,0:T(8,128)(2,1)} %bitcast.417, ...), kind=kOutput, calls=%fused_computation.136.clone.1 | convolution fusion | flops 157484160 | bytes 3753992 | tf_op jit(solution)/shard_map/while/body/eval_jaxpr/sub | solution.py:23
  182.3 2.7 fusion.122
  202.6 4.2 %fusion.120 = (f32[4,128]{1,0:T(4,128)S(1)}, f32[4,128,1152]{2,1,0:T(8,128)}) fusion(s32[4,128]{1,0:T(4,128)S(1)} %get-tuple-element.431, s32[4,1152]{1,0:T(4,128)S(1)} %bitcast.432, s32[4,128]{1,0:T(4,128)S(1)} %iota_add_fusion.5, s32[4,1152]{1,0:T(4,128)S(1)} %iota_add_fusion.6, bf16[4,1152,128]{2,1,0:T(8,128)(2,1)} %bitcast.417, ...), kind=kOutput, calls=%fused_computation.136.clone.1 | convolution fusion | flops 157484160 | bytes 3753992 | tf_op jit(solution)/shard_map/while/body/eval_jaxpr/sub | solution.py:23
  206.8 2.7 fusion.122
  227.1 4.3 %fusion.120 = (f32[4,128]{1,0:T(4,128)S(1)}, f32[4,128,1152]{2,1,0:T(8,128)}) fusion(s32[4,128]{1,0:T(4,128)S(1)} %get-tuple-element.431, s32[4,1152]{1,0:T(4,128)S(1)} %bitcast.432, s32[4,128]{1,0:T(4,128)S(1)} %iota_add_fusion.5, s32[4,1152]{1,0:T(4,128)S(1)} %iota_add_fusion.6, bf16[4,1152,128]{2,1,0:T(8,128)(2,1)} %bitcast.417, ...), kind=kOutput, calls=%fused_computation.136.clone.1 | convolution fusion | flops 157484160 | bytes 3753992 | tf_op jit(solution)/shard_map/while/body/eval_jaxpr/sub | solution.py:23
  231.4 2.7 fusion.122
  251.7 4.2 %fusion.120 = (f32[4,128]{1,0:T(4,128)S(1)}, f32[4,128,1152]{2,1,0:T(8,128)}) fusion(s32[4,128]{1,0:T(4,128)S(1)} %get-tuple-element.431, s32[4,1152]{1,0:T(4,128)S(1)} %bitcast.432, s32[4,128]{1,0:T(4,128)S(1)} %iota_add_fusion.5, s32[4,1152]{1,0:T(4,128)S(1)} %iota_add_fusion.6, bf16[4,1152,128]{2,1,0:T(8,128)(2,1)} %bitcast.417, ...), kind=kOutput, calls=%fused_computation.136.clone.1 | convolution fusion | flops 157484160 | bytes 3753992 | tf_op jit(solution)/shard_map/while/body/eval_jaxpr/sub | solution.py:23
  255.9 2.7 fusion.122
  276.2 4.3 %fusion.120 = (f32[4,128]{1,0:T(4,128)S(1)}, f32[4,128,1152]{2,1,0:T(8,128)}) fusion(s32[4,128]{1,0:T(4,128)S(1)} %get-tuple-element.431, s32[4,1152]{1,0:T(4,128)S(1)} %bitcast.432, s32[4,128]{1,0:T(4,128)S(1)} %iota_add_fusion.5, s32[4,1152]{1,0:T(4,128)S(1)} %iota_add_fusion.6, bf16[4,1152,128]{2,1,0:T(8,128)(2,1)} %bitcast.417, ...), kind=kOutput, calls=%fused_computation.136.clone.1 | convolution fusion | flops 157484160 | bytes 3753992 | tf_op jit(solution)/shard_map/while/body/eval_jaxpr/sub | solution.py:23
  280.5 2.7 fusion.122
  300.8 4.2 %fusion.120 = (f32[4,128]{1,0:T(4,128)S(1)}, f32[4,128,1152]{2,1,0:T(8,128)}) fusion(s32[4,128]{1,0:T(4,128)S(1)} %get-tuple-element.431, s32[4,1152]{1,0:T(4,128)S(1)} %bitcast.432, s32[4,128]{1,0:T(4,128)S(1)} %iota_add_fusion.5, s32[4,1152]{1,0:T(4,128)S(1)} %iota_add_fusion.6, bf16[4,1152,128]{2,1,0:T(8,128)(2,1)} %bitcast.417, ...), kind=kOutput, calls=%fused_computation.136.clone.1 | convolution fusion | flops 157484160 | bytes 3753992 | tf_op jit(solution)/shard_map/while/body/eval_jaxpr/sub | solution.py:23
  305.0 2.7 fusion.122
  313.6 3.3 copy.143
  316.9 17.2 %all-to-all-start.2 = ((bf16[128,16,2,128]{3,2,0,1:T(2,128)(2,1)}), bf16[128,16,2,128]{3,2,0,1:T(2,128)(2,1)}, u32[]{:S(2)}, u32[]{:S(2)}) async-start(bf16[128,16,2,128]{3,2,0,1:T(2,128)(2,1)} %copy.143), calls=%async_computation.2 | async-start | bytes 2097152 | tf_op jit(solution)/shard_map/all_to_all | solution.py:159
  335.7 21.4 %all-to-all-done.2 = bf16[128,16,2,128]{3,2,0,1:T(2,128)(2,1)} async-done(((bf16[128,16,2,128]{3,2,0,1:T(2,128)(2,1)}), bf16[128,16,2,128]{3,2,0,1:T(2,128)(2,1)}, u32[]{:S(2)}, u32[]{:S(2)}) %all-to-all-start.2) | async-done | bytes 1048608 | tf_op jit(solution)/shard_map/all_to_all | solution.py:159
  357.1 6.9 %all-to-all-start.3 = ((f32[2,16,1,128,128]{4,3,0,2,1:T(8,128)}), f32[2,16,1,128,128]{4,3,0,2,1:T(8,128)S(1)}, u32[]{:S(2)}, u32[]{:S(2)}) async-start(f32[2,16,1,128,128]{4,3,0,2,1:T(8,128)} %maximum_bitcast_fusion), calls=%async_computation.3 | async-start | bytes 4194304 | tf_op jit(solution)/shard_map/all_to_all | solution.py:168
  364.0 2.5 copy.144
  367.8 37.3 %all-to-all-done.3 = f32[2,16,1,128,128]{4,3,0,2,1:T(8,128)S(1)} async-done(((f32[2,16,1,128,128]{4,3,0,2,1:T(8,128)}), f32[2,16,1,128,128]{4,3,0,2,1:T(8,128)S(1)}, u32[]{:S(2)}, u32[]{:S(2)}) %all-to-all-start.3) | async-done | bytes 2097184 | tf_op jit(solution)/shard_map/all_to_all | solution.py:168
  (507 shorter events, 130.9 us)
Async XLA Ops:
  2.8 8.8 %copy-start.4 = (bf16[128,4096]{1,0:T(8,128)(2,1)S(1)}, bf16[128,4096]{1,0:T(8,128)(2,1)}, u32[]{:S(2)}) copy-start(bf16[128,4096]{1,0:T(8,128)(2,1)} %param.8) | copy-start | bytes 3145732
  4.0 8.9 %copy-start.5 = (bf16[128,4096]{1,0:T(8,128)(2,1)S(1)}, bf16[128,4096]{1,0:T(8,128)(2,1)}, u32[]{:S(2)}) copy-start(bf16[128,4096]{1,0:T(8,128)(2,1)} %param.11) | copy-start | bytes 3145732
  4.0 30.5 %all-to-all-start.1 = ((bf16[2,128,16,128]{3,1,0,2:T(8,128)(2,1)}), bf16[2,128,16,128]{3,1,0,2:T(8,128)(2,1)}, u32[]{:S(2)}, u32[]{:S(2)}) async-start(bf16[2,128,16,128]{3,1,0,2:T(8,128)(2,1)} %bitcast.11), calls=%async_computation.1 | async-start | bytes 2097152 | tf_op jit(solution)/shard_map/all_to_all | solution.py:82
  19.7 21.7 %copy-start.8 = (s32[128]{0:T(128)S(1)}, s32[128]{0:T(128)}, u32[]{:S(2)}) copy-start(s32[128]{0:T(128)} %param.13) | copy-start | bytes 1540
  34.5 76.6 %all-to-all-start = ((bf16[3,128,32,128]{1,3,0,2:T(8,128)(2,1)}), bf16[3,128,32,128]{1,3,0,2:T(8,128)(2,1)}, u32[]{:S(2)}, u32[]{:S(2)}) async-start(bf16[3,128,32,128]{1,3,0,2:T(8,128)(2,1)} %copy.136), calls=%async_computation | async-start | bytes 6291456 | tf_op jit(solution)/shard_map/all_to_all | solution.py:67
  120.7 5.7 %copy-start = (bf16[24,128,128]{2,1,0:T(8,128)(2,1)S(1)}, bf16[24,128,128]{2,1,0:T(8,128)(2,1)}, u32[]{:S(2)}) copy-start(bf16[24,128,128]{2,1,0:T(8,128)(2,1)} %get-tuple-element.515) | copy-start | bytes 2359300 | tf_op jit(solution)/shard_map/while
  120.7 6.9 %copy-start.1 = (bf16[24,128,128]{2,1,0:T(8,128)(2,1)S(1)}, bf16[24,128,128]{2,1,0:T(8,128)(2,1)}, u32[]{:S(2)}) copy-start(bf16[24,128,128]{2,1,0:T(8,128)(2,1)} %get-tuple-element.513) | copy-start | bytes 2359300 | tf_op jit(solution)/shard_map/while
  133.2 2.7 copy-start.3
  135.9 1.7 copy-start.9
  145.3 5.7 %copy-start = (bf16[24,128,128]{2,1,0:T(8,128)(2,1)S(1)}, bf16[24,128,128]{2,1,0:T(8,128)(2,1)}, u32[]{:S(2)}) copy-start(bf16[24,128,128]{2,1,0:T(8,128)(2,1)} %get-tuple-element.515) | copy-start | bytes 2359300 | tf_op jit(solution)/shard_map/while
  145.3 6.9 %copy-start.1 = (bf16[24,128,128]{2,1,0:T(8,128)(2,1)S(1)}, bf16[24,128,128]{2,1,0:T(8,128)(2,1)}, u32[]{:S(2)}) copy-start(bf16[24,128,128]{2,1,0:T(8,128)(2,1)} %get-tuple-element.513) | copy-start | bytes 2359300 | tf_op jit(solution)/shard_map/while
  157.7 2.7 copy-start.3
  169.8 5.7 %copy-start = (bf16[24,128,128]{2,1,0:T(8,128)(2,1)S(1)}, bf16[24,128,128]{2,1,0:T(8,128)(2,1)}, u32[]{:S(2)}) copy-start(bf16[24,128,128]{2,1,0:T(8,128)(2,1)} %get-tuple-element.515) | copy-start | bytes 2359300 | tf_op jit(solution)/shard_map/while
  169.8 6.9 %copy-start.1 = (bf16[24,128,128]{2,1,0:T(8,128)(2,1)S(1)}, bf16[24,128,128]{2,1,0:T(8,128)(2,1)}, u32[]{:S(2)}) copy-start(bf16[24,128,128]{2,1,0:T(8,128)(2,1)} %get-tuple-element.513) | copy-start | bytes 2359300 | tf_op jit(solution)/shard_map/while
  182.3 2.7 copy-start.3
  194.4 5.7 %copy-start = (bf16[24,128,128]{2,1,0:T(8,128)(2,1)S(1)}, bf16[24,128,128]{2,1,0:T(8,128)(2,1)}, u32[]{:S(2)}) copy-start(bf16[24,128,128]{2,1,0:T(8,128)(2,1)} %get-tuple-element.515) | copy-start | bytes 2359300 | tf_op jit(solution)/shard_map/while
  194.4 6.9 %copy-start.1 = (bf16[24,128,128]{2,1,0:T(8,128)(2,1)S(1)}, bf16[24,128,128]{2,1,0:T(8,128)(2,1)}, u32[]{:S(2)}) copy-start(bf16[24,128,128]{2,1,0:T(8,128)(2,1)} %get-tuple-element.513) | copy-start | bytes 2359300 | tf_op jit(solution)/shard_map/while
  206.8 2.7 copy-start.3
  218.9 5.7 %copy-start = (bf16[24,128,128]{2,1,0:T(8,128)(2,1)S(1)}, bf16[24,128,128]{2,1,0:T(8,128)(2,1)}, u32[]{:S(2)}) copy-start(bf16[24,128,128]{2,1,0:T(8,128)(2,1)} %get-tuple-element.515) | copy-start | bytes 2359300 | tf_op jit(solution)/shard_map/while
  218.9 6.9 %copy-start.1 = (bf16[24,128,128]{2,1,0:T(8,128)(2,1)S(1)}, bf16[24,128,128]{2,1,0:T(8,128)(2,1)}, u32[]{:S(2)}) copy-start(bf16[24,128,128]{2,1,0:T(8,128)(2,1)} %get-tuple-element.513) | copy-start | bytes 2359300 | tf_op jit(solution)/shard_map/while
  231.4 2.7 copy-start.3
  243.5 5.7 %copy-start = (bf16[24,128,128]{2,1,0:T(8,128)(2,1)S(1)}, bf16[24,128,128]{2,1,0:T(8,128)(2,1)}, u32[]{:S(2)}) copy-start(bf16[24,128,128]{2,1,0:T(8,128)(2,1)} %get-tuple-element.515) | copy-start | bytes 2359300 | tf_op jit(solution)/shard_map/while
  243.5 6.9 %copy-start.1 = (bf16[24,128,128]{2,1,0:T(8,128)(2,1)S(1)}, bf16[24,128,128]{2,1,0:T(8,128)(2,1)}, u32[]{:S(2)}) copy-start(bf16[24,128,128]{2,1,0:T(8,128)(2,1)} %get-tuple-element.513) | copy-start | bytes 2359300 | tf_op jit(solution)/shard_map/while
  255.9 2.7 copy-start.3
  268.0 5.7 %copy-start = (bf16[24,128,128]{2,1,0:T(8,128)(2,1)S(1)}, bf16[24,128,128]{2,1,0:T(8,128)(2,1)}, u32[]{:S(2)}) copy-start(bf16[24,128,128]{2,1,0:T(8,128)(2,1)} %get-tuple-element.515) | copy-start | bytes 2359300 | tf_op jit(solution)/shard_map/while
  268.0 6.9 %copy-start.1 = (bf16[24,128,128]{2,1,0:T(8,128)(2,1)S(1)}, bf16[24,128,128]{2,1,0:T(8,128)(2,1)}, u32[]{:S(2)}) copy-start(bf16[24,128,128]{2,1,0:T(8,128)(2,1)} %get-tuple-element.513) | copy-start | bytes 2359300 | tf_op jit(solution)/shard_map/while
  280.5 2.7 copy-start.3
  292.6 5.7 %copy-start = (bf16[24,128,128]{2,1,0:T(8,128)(2,1)S(1)}, bf16[24,128,128]{2,1,0:T(8,128)(2,1)}, u32[]{:S(2)}) copy-start(bf16[24,128,128]{2,1,0:T(8,128)(2,1)} %get-tuple-element.515) | copy-start | bytes 2359300 | tf_op jit(solution)/shard_map/while
  292.6 6.9 %copy-start.1 = (bf16[24,128,128]{2,1,0:T(8,128)(2,1)S(1)}, bf16[24,128,128]{2,1,0:T(8,128)(2,1)}, u32[]{:S(2)}) copy-start(bf16[24,128,128]{2,1,0:T(8,128)(2,1)} %get-tuple-element.513) | copy-start | bytes 2359300 | tf_op jit(solution)/shard_map/while
  305.0 2.7 copy-start.3
  316.9 40.2 %all-to-all-start.2 = ((bf16[128,16,2,128]{3,2,0,1:T(2,128)(2,1)}), bf16[128,16,2,128]{3,2,0,1:T(2,128)(2,1)}, u32[]{:S(2)}, u32[]{:S(2)}) async-start(bf16[128,16,2,128]{3,2,0,1:T(2,128)(2,1)} %copy.143), calls=%async_computation.2 | async-start | bytes 2097152 | tf_op jit(solution)/shard_map/all_to_all | solution.py:159
  357.1 48.0 %all-to-all-start.3 = ((f32[2,16,1,128,128]{4,3,0,2,1:T(8,128)}), f32[2,16,1,128,128]{4,3,0,2,1:T(8,128)S(1)}, u32[]{:S(2)}, u32[]{:S(2)}) async-start(f32[2,16,1,128,128]{4,3,0,2,1:T(8,128)} %maximum_bitcast_fusion), calls=%async_computation.3 | async-start | bytes 4194304 | tf_op jit(solution)/shard_map/all_to_all | solution.py:168
  (24 other events, 29.9 us)
where the time goes:
time: 415 us; the launch traced here: 407 us
  local copies, waits for them, and re-layouts  101 us (24%)
  matrix products  89.7 us (22%)
  waiting for transfers between devices  73.5 us (18%)
  blocking collectives  67 us (16%)
  starting transfers between devices  38.5 us (9%)
  loops' own time  23.9 us (6%)
  other arithmetic  12.9 us (3%)
    while x232, local copies, waits for them, and re-layouts  68.7 us
    all_gather x1, blocking collectives, by_heads(): doc_full = lax.all_gather(doc_ids, 'ctx', axis=0, tiled=True)  67 us
    all_to_all x1, waiting for transfers between devices, by_heads(): lax.all_to_all(grad_pair, 'ctx', split_axis=1, concat_axis=2, tiled=True)  37.3 us
    sub x8, matrix products, attend(): raw_weights = jnp.where(visible, jnp.exp(scores - row_max), 0.0)  34 us
    another operation x1, loops' own time, by_heads(): lax.scan(one_group, (empty, empty), jnp.arange(work_total, dtype=jnp.int32))  23.9 us
    dot_general x8, matrix products, attend(): jnp.einsum('its,ios->ito', gradient_tile, value_window_slice, preferred_e...  21.7 us
    all_to_all x1, waiting for transfers between devices, by_heads(): lax.all_to_all(query_back, 'ctx', split_axis=1, concat_axis=2, tiled=True)  21.4 us
    all_to_all x1, starting transfers between devices, by_heads(): lax.all_to_all(query_back, 'ctx', split_axis=1, concat_axis=2, tiled=True)  17.2 us
  transfers between devices with their start and end apart: 4, of which 3 were waited for; matrix products, arithmetic and copies ran while one was open for 4% of the time, Pallas kernels for 0%

commit v1 on v0

v1 whole, which is shorter than its diff:
```python
import functools
import math

import jax
import jax.numpy as jnp
from jax import lax
from jax.experimental import pallas as pl
from jax.experimental.pallas import tpu as pltpu
from jax.sharding import PartitionSpec as P

HEAD_DIM = 128
HEADS = 32
KV_HEADS = 4
BLOCKS = 9
EVENS = 5
PAIRS = 4
DOC_ROWS = 16


def to(rank):
    return dict(device_id={"ctx": rank}, device_id_type=pl.DeviceIdType.MESH)


def kernel(
    ranks,
    q_ref,
    k_ref,
    v_ref,
    g_ref,
    o_ref,
    doc_ref,
    dq_ref,
    dk_ref,
    dv_ref,
    win,
    bias,
    acc_k,
    acc_v,
    sum_k,
    sum_v,
    sib_out,
    sib_in,
    x_out,
    x_in,
    z_out,
    z_in,
    in_send,
    in_recv,
    back_send,
    back_recv,
):
    rows = q_ref.shape[0]
    span = BLOCKS * rows
    scale = 1.0 / math.sqrt(HEAD_DIM)
    exp_scale = scale * math.log2(math.e)
    rank = lax.axis_index("ctx")
    core = rank % 2
    col = (rank // 2) % 2
    sibling = rank + 1 - 2 * core
    partner = rank + 2 - 4 * col
    up4, up8 = rank + 4 < ranks, rank + 8 < ranks
    down4, down8 = rank >= 4, rank >= 8

    barrier = pltpu.get_barrier_semaphore()
    for peer in (sibling, partner):
        pl.semaphore_signal(barrier, inc=1, **to(peer))
    for there, peer in ((up4, rank + 4), (up8, rank + 8), (down4, rank - 4), (down8, rank - 8)):

        @pl.when(there)
        def _(peer=peer):
            pl.semaphore_signal(barrier, inc=1, **to(peer))

    own_doc = doc_ref[...].astype(jnp.float32)
    for g in range(KV_HEADS):
        cols = slice(g * HEAD_DIM, (g + 1) * HEAD_DIM)
        win[g, 0, 0:rows, :] = k_ref[:, cols]
        win[g, 0, rows : 2 * rows, :] = v_ref[:, cols]
        win[g, 0, 2 * rows :, :] = jnp.broadcast_to(own_doc, (DOC_ROWS, rows)).astype(jnp.bfloat16)
        for slot, there in ((2, down4), (4, down8)):

            @pl.when(jnp.logical_not(there))
            def _(g=g, slot=slot):
                win[g, slot, 0 : 2 * rows, :] = jnp.zeros((2 * rows, HEAD_DIM), jnp.bfloat16)
                win[g, slot, 2 * rows :, :] = jnp.full((DOC_ROWS, HEAD_DIM), -1.0, jnp.bfloat16)

    near = [there.astype(jnp.int32) for there in (up4, up8, down4, down8)]
    pl.semaphore_wait(barrier, 2 + sum(near))

    def in_z(g, step):
        return pltpu.make_async_remote_copy(
            src_ref=win.at[g, 0],
            dst_ref=win.at[g, 2 * step],
            send_sem=in_send.at[g, step - 1],
            recv_sem=in_recv.at[g, step - 1],
            **to(rank + 4 * step),
        )

    def in_x(g, half):
        return pltpu.make_async_remote_copy(
            src_ref=win.at[g, 2 * col + 2 * half],
            dst_ref=win.at[g, 1 + 2 * half],
            send_sem=in_send.at[g, 2 + half],
            recv_sem=in_recv.at[g, 2 + half],
            **to(partner),
        )

    def in_sib(g):
        return pltpu.make_async_remote_copy(
            src_ref=win.at[g, pl.ds(core, 4)],
            dst_ref=win.at[g, pl.ds(EVENS, 4)],
            send_sem=in_send.at[g, 4],
            recv_sem=in_recv.at[g, 4],
            **to(sibling),
        )

    def start_z(g):
        @pl.when(up4)
        def _():
            in_z(g, 1).start()

        @pl.when(up8)
        def _():
            in_z(g, 2).start()

    def start_x(g):
        @pl.when(down4)
        def _():
            in_z(g, 1).wait_recv()

        @pl.when(down8)
        def _():
            in_z(g, 2).wait_recv()

        in_x(g, 0).start()
        in_x(g, 1).start()

    def start_sib(g):
        in_x(g, 0).wait_recv()
        in_x(g, 1).wait_recv()
        in_sib(g).start()

    def back_sib(g):
        return pltpu.make_async_remote_copy(
            src_ref=sib_out.at[g],
            dst_ref=sib_in.at[g],
            send_sem=back_send.at[g, 0],
            recv_sem=back_recv.at[g, 0],
            **to(sibling),
        )

    def back_x(g):
        return pltpu.make_async_remote_copy(
            src_ref=x_out.at[g],
            dst_ref=x_in.at[g],
            send_sem=back_send.at[g, 1],
            recv_sem=back_recv.at[g, 1],
            **to(partner),
        )

    def back_z(g, step):
        return pltpu.make_async_remote_copy(
            src_ref=z_out.at[g, step - 1],
            dst_ref=z_in.at[g, step - 1],
            send_sem=back_send.at[g, 1 + step],
            recv_sem=back_recv.at[g, 1 + step],
            **to(rank - 4 * step),
        )

    def stage_sib(g):
        for j in range(4):
            sib_out[g, j, 0:rows, :] = acc_k[EVENS + j].astype(jnp.bfloat16)
            sib_out[g, j, rows:, :] = acc_v[EVENS + j].astype(jnp.bfloat16)
        back_sib(g).start()
        sum_k[...] = acc_k[0:EVENS]
        sum_v[...] = acc_v[0:EVENS]

    def stage_x(g):
        back_sib(g).wait_recv()
        for j in range(4):
            sum_k[core + j] += sib_in[g, j, 0:rows, :].astype(jnp.float32)
            sum_v[core + j] += sib_in[g, j, rows:, :].astype(jnp.float32)
        for half in range(2):
            x_out[g, half, 0:rows, :] = sum_k[1 + 2 * half].astype(jnp.bfloat16)
            x_out[g, half, rows:, :] = sum_v[1 + 2 * half].astype(jnp.bfloat16)
        back_x(g).start()

    def stage_z(g):
        back_x(g).wait_recv()
        for half in range(2):
            slot = 2 * col + 2 * half
            sum_k[slot] += x_in[g, half, 0:rows, :].astype(jnp.float32)
            sum_v[slot] += x_in[g, half, rows:, :].astype(jnp.float32)
        for step, there in ((1, down4), (2, down8)):
            z_out[g, step - 1, 0:rows, :] = sum_k[2 * step].astype(jnp.bfloat16)
            z_out[g, step - 1, rows:, :] = sum_v[2 * step].astype(jnp.bfloat16)

            @pl.when(there)
            def _(step=step):
                back_z(g, step).start()

    def finish(g):
        for step, there in ((1, up4), (2, up8)):

            @pl.when(there)
            def _(step=step):
                back_z(g, step).wait_recv()
                sum_k[0] += z_in[g, step - 1, 0:rows, :].astype(jnp.float32)
                sum_v[0] += z_in[g, step - 1, rows:, :].astype(jnp.float32)

        cols = pl.ds(pl.multiple_of(g * HEAD_DIM, HEAD_DIM), HEAD_DIM)
        dk_ref[:, cols] = (sum_k[0] * scale).astype(jnp.bfloat16)
        dv_ref[:, cols] = sum_v[0].astype(jnp.bfloat16)

    for g in range(KV_HEADS):
        start_z(g)
    start_x(0)
    start_sib(0)
    start_x(1)
    in_sib(0).wait_recv()

    row_no = lax.broadcasted_iota(jnp.int32, (rows, rows), 0)
    col_no = lax.broadcasted_iota(jnp.int32, (rows, rows), 1)
    for slot in range(BLOCKS):
        line = win[0, slot, 2 * rows :, :].astype(jnp.float32)[0:1]
        key_doc = jnp.broadcast_to(line, (rows, rows)).T
        seen = key_doc == own_doc
        if slot == 0:
            seen = seen & (row_no <= col_no)
        bias[slot * rows : (slot + 1) * rows, :] = jnp.where(seen, 0.0, -1e30)

    def step(t, carry):
        g, pair = t // PAIRS, t % PAIRS

        @pl.when((pair == 0) & (g > 0))
        def _():
            in_sib(g).wait_recv()

        @pl.when((pair == 0) & (g < KV_HEADS - 1))
        def _():
            start_sib(g + 1)

        @pl.when((pair == 2) & (g < KV_HEADS - 2))
        def _():
            start_x(g + 2)

        @pl.when(pair == 0)
        def _():
            acc_k[...] = jnp.zeros_like(acc_k)
            acc_v[...] = jnp.zeros_like(acc_v)

        first = pl.ds(pl.multiple_of(t * 2 * HEAD_DIM, HEAD_DIM), HEAD_DIM)
        second = pl.ds(pl.multiple_of(t * 2 * HEAD_DIM + HEAD_DIM, HEAD_DIM), HEAD_DIM)
        q = jnp.concatenate([q_ref[:, first], q_ref[:, second]], axis=0)
        grad = jnp.concatenate([g_ref[:, first], g_ref[:, second]], axis=0)
        out = jnp.concatenate([o_ref[:, first], o_ref[:, second]], axis=0)
        delta = jnp.sum((grad.astype(jnp.float32) * out.astype(jnp.float32)).T, axis=0, keepdims=True)
        keys = win[g, :, 0:rows, :].reshape(span, HEAD_DIM)
        vals = win[g, :, rows : 2 * rows, :].reshape(span, HEAD_DIM)
        nt = (((1,), (1,)), ((), ()))
        scores = lax.dot_general(keys, q, nt, preferred_element_type=jnp.float32)
        mask = bias[...]
        scores = scores + jnp.concatenate([mask, mask], axis=1)
        top = jnp.max(scores, axis=0, keepdims=True)
        raw = jnp.exp2((scores - top) * exp_scale)
        prob = raw * (1.0 / jnp.sum(raw, axis=0, keepdims=True))
        prob_grad = lax.dot_general(vals, grad, nt, preferred_element_type=jnp.float32)
        low = (prob * (prob_grad - delta)).astype(jnp.bfloat16)
        acc_v[...] += jnp.dot(
            prob.astype(jnp.bfloat16), grad, preferred_element_type=jnp.float32
        ).reshape(BLOCKS, rows, HEAD_DIM)
        acc_k[...] += jnp.dot(low, q, preferred_element_type=jnp.float32).reshape(
            BLOCKS, rows, HEAD_DIM
        )
        tn = (((0,), (0,)), ((), ()))
        dq = lax.dot_general(low, keys, tn, preferred_element_type=jnp.float32) * scale
        dq = dq.astype(jnp.bfloat16)
        dq_ref[:, first] = dq[0:rows]
        dq_ref[:, second] = dq[rows:]

        @pl.when((pair == 0) & (g > 0))
        def _():
            stage_x(g - 1)

        @pl.when((pair == 1) & (g > 0))
        def _():
            stage_z(g - 1)

        @pl.when((pair == 3) & (g > 0))
        def _():
            finish(g - 1)

        @pl.when(pair == 3)
        def _():
            stage_sib(g)

        return carry

    lax.fori_loop(0, KV_HEADS * PAIRS, step, 0)
    last = KV_HEADS - 1
    stage_x(last)
    stage_z(last)
    finish(last)
    for g in range(KV_HEADS):
        in_x(g, 0).wait_send()
        in_x(g, 1).wait_send()
        in_sib(g).wait_send()
        back_sib(g).wait_send()
        back_x(g).wait_send()
        for n, there_in, there_out in ((1, up4, down4), (2, up8, down8)):

            @pl.when(there_in)
            def _(g=g, n=n):
                in_z(g, n).wait_send()

            @pl.when(there_out)
            def _(g=g, n=n):
                back_z(g, n).wait_send()


def on_device(queries, keys, values, out_grad, attn_out, doc_ids):
    ranks = lax.axis_size("ctx")
    rows = queries.shape[0]
    bf16, f32 = jnp.bfloat16, jnp.float32
    vmem = pl.BlockSpec(memory_space=pltpu.VMEM)
    block = (rows, HEAD_DIM)
    pair = (2 * rows, HEAD_DIM)
    return pl.pallas_call(
        functools.partial(kernel, ranks),
        out_shape=(
            jax.ShapeDtypeStruct(queries.shape, bf16),
            jax.ShapeDtypeStruct(keys.shape, bf16),
            jax.ShapeDtypeStruct(values.shape, bf16),
        ),
        in_specs=[vmem] * 6,
        out_specs=(vmem,) * 3,
        scratch_shapes=[
            pltpu.VMEM((KV_HEADS, BLOCKS, 2 * rows + DOC_ROWS, HEAD_DIM), bf16),
            pltpu.VMEM((BLOCKS * rows, rows), f32),
            pltpu.VMEM((BLOCKS,) + block, f32),
            pltpu.VMEM((BLOCKS,) + block, f32),
            pltpu.VMEM((EVENS,) + block, f32),
            pltpu.VMEM((EVENS,) + block, f32),
            pltpu.VMEM((KV_HEADS, 4) + pair, bf16),
            pltpu.VMEM((KV_HEADS, 4) + pair, bf16),
            pltpu.VMEM((KV_HEADS, 2) + pair, bf16),
            pltpu.VMEM((KV_HEADS, 2) + pair, bf16),
            pltpu.VMEM((KV_HEADS, 2) + pair, bf16),
            pltpu.VMEM((KV_HEADS, 2) + pair, bf16),
            pltpu.SemaphoreType.DMA((KV_HEADS, 5)),
            pltpu.SemaphoreType.DMA((KV_HEADS, 5)),
            pltpu.SemaphoreType.DMA((KV_HEADS, 4)),
            pltpu.SemaphoreType.DMA((KV_HEADS, 4)),
        ],
        compiler_params=pltpu.CompilerParams(
            collective_id=0, has_side_effects=True, vmem_limit_bytes=48 * 1024 * 1024
        ),
    )(queries, keys, values, out_grad, attn_out, doc_ids.reshape(1, rows))


def solution(mesh):
    spec = P(("groups", "ctx"), None)
    return jax.shard_map(
        on_device,
        mesh=mesh,
        in_specs=(spec,) * 5 + (P(("groups", "ctx")),),
        out_specs=(spec,) * 3,
        check_vma=False,
    )
```

time: 415 us -> 81.2 us (0.20); the launches traced: 407 us -> 80.9 us
  local copies, waits for them, and re-layouts: 101 us -> 8.41 us
  matrix products: 89.7 us -> 0 us
  waiting for transfers between devices: 73.5 us -> 0 us
  Pallas kernels: 0 us -> 71.8 us
  blocking collectives: 67 us -> 0 us
  starting transfers between devices: 38.5 us -> 0 us
  loops' own time: 23.9 us -> 0 us
  other arithmetic: 12.9 us -> 0 us
    all_to_all x4 -> x0, waiting for transfers between devices: 73.5 us -> none  [the longest x1 37.3 us: by_heads(): lax.all_to_all(grad_pair, 'ctx', split_axis=1, concat_axis=2, tiled=True)]
    pallas_call x0 -> x1, Pallas kernels: none -> 71.8 us  [on_device(): pl.pallas_call(functools.partial(kernel, ranks), out_shape=(jax.ShapeDtyp...]
    while x232 -> x0, local copies, waits for them, and re-layouts: 68.7 us -> none
    all_gather x1 -> x0, blocking collectives: 67 us -> none  [by_heads(): doc_full = lax.all_gather(doc_ids, 'ctx', axis=0, tiled=True)]
    dot_general x32 -> x0, matrix products: 55.6 us -> none  [the longest x8 21.7 us: attend(): jnp.einsum('its,ios->ito', gradient_tile, value_window_slice, preferred_e...]
    all_to_all x4 -> x0, starting transfers between devices: 38.5 us -> none  [the longest x1 17.2 us: by_heads(): lax.all_to_all(query_back, 'ctx', split_axis=1, concat_axis=2, tiled=True)]
    sub x8 -> x0, matrix products: 34 us -> none  [attend(): raw_weights = jnp.where(visible, jnp.exp(scores - row_max), 0.0)]
    another operation x1 -> x0, loops' own time: 23.9 us -> none  [by_heads(): lax.scan(one_group, (empty, empty), jnp.arange(work_total, dtype=jnp.int32))]
  transfers between devices with their start and end apart: 4 -> 0, of which waited for: 3 -> 0; matrix products, arithmetic and copies ran while one was open for 4% -> 0% of each run, Pallas kernels for 0% -> 0%
where the time goes in v1:
time: 81.2 us; the launch traced here: 80.9 us
  Pallas kernels  71.8 us (88%)
  local copies, waits for them, and re-layouts  8.41 us (10%)
    pallas_call x1, Pallas kernels, on_device(): pl.pallas_call(functools.partial(kernel, ranks), out_shape=(jax.ShapeDtyp...  71.8 us
    unnamed x15, local copies, waits for them, and re-layouts  8.41 us

profile of v1, /device:TPU:0, one launch (start us, length us, event | category | flops | bytes accessed | tf_op | source)
XLA Modules:
  0.0 80.9 jit_solution(16483485389588919725)
XLA Ops:
  0.6 0.0 copy-start.5
  0.6 0.6 copy-done.5
  1.3 0.0 copy-start
  1.3 1.2 %copy-done = bf16[128,4096]{1,0:T(8,128)(2,1)S(1)} copy-done((bf16[128,4096]{1,0:T(8,128)(2,1)S(1)}, bf16[128,4096]{1,0:T(8,128)(2,1)}, u32[]{:S(2)}) %copy-start) | copy-done | bytes 1048600
  2.5 0.0 copy-start.1
  2.5 1.2 %copy-done.1 = bf16[128,4096]{1,0:T(8,128)(2,1)S(1)} copy-done((bf16[128,4096]{1,0:T(8,128)(2,1)S(1)}, bf16[128,4096]{1,0:T(8,128)(2,1)}, u32[]{:S(2)}) %copy-start.1) | copy-done | bytes 1048600
  3.7 0.0 copy-start.2
  3.7 1.2 %copy-done.2 = bf16[128,4096]{1,0:T(8,128)(2,1)S(1)} copy-done((bf16[128,4096]{1,0:T(8,128)(2,1)S(1)}, bf16[128,4096]{1,0:T(8,128)(2,1)}, u32[]{:S(2)}) %copy-start.2) | copy-done | bytes 1048600
  5.0 0.0 copy-start.3
  5.0 0.9 %copy-done.3 = bf16[128,512]{1,0:T(8,128)(2,1)S(1)} copy-done((bf16[128,512]{1,0:T(8,128)(2,1)S(1)}, bf16[128,512]{1,0:T(8,128)(2,1)}, u32[]{:S(2)}) %copy-start.3) | copy-done | bytes 131096
  5.9 0.0 copy-start.4
  5.9 0.9 %copy-done.4 = bf16[128,512]{1,0:T(8,128)(2,1)S(1)} copy-done((bf16[128,512]{1,0:T(8,128)(2,1)S(1)}, bf16[128,512]{1,0:T(8,128)(2,1)}, u32[]{:S(2)}) %copy-start.4) | copy-done | bytes 131096
  6.8 71.8 %shard_map.85 = (bf16[128,4096]{1,0:T(8,128)(2,1)S(1)}, bf16[128,512]{1,0:T(8,128)(2,1)S(1)}, bf16[128,512]{1,0:T(8,128)(2,1)S(1)}) custom-call(bf16[128,4096]{1,0:T(8,128)(2,1)S(1)} %copy-done, bf16[128,512]{1,0:T(8,128)(2,1)S(1)} %copy-done.3, bf16[128,512]{1,0:T(8,128)(2,1)S(1)} %copy-done.4, bf16[128,4096]{1,0:T(8,128)(2,1)S(1)} %copy-done.1, ...), custom_call_target="tpu_custom_call" | custom-call | tf_op jit(solution)/shard_map/pallas_call | solution.py:327
  78.6 1.0 %copy.12 = bf16[128,4096]{1,0:T(8,128)(2,1)} copy(bf16[128,4096]{1,0:T(8,128)(2,1)S(1)} %get-tuple-element.6) | data formatting | bytes 2097152
  79.6 0.7 copy.13
  80.2 0.7 copy.14
Async XLA Ops:
  0.6 0.7 copy-start.5
  1.3 1.2 %copy-start = (bf16[128,4096]{1,0:T(8,128)(2,1)S(1)}, bf16[128,4096]{1,0:T(8,128)(2,1)}, u32[]{:S(2)}) copy-start(bf16[128,4096]{1,0:T(8,128)(2,1)} %q_ref.1) | copy-start | bytes 3145732
  2.5 1.2 %copy-start.1 = (bf16[128,4096]{1,0:T(8,128)(2,1)S(1)}, bf16[128,4096]{1,0:T(8,128)(2,1)}, u32[]{:S(2)}) copy-start(bf16[128,4096]{1,0:T(8,128)(2,1)} %g_ref.1) | copy-start | bytes 3145732
  3.7 1.2 %copy-start.2 = (bf16[128,4096]{1,0:T(8,128)(2,1)S(1)}, bf16[128,4096]{1,0:T(8,128)(2,1)}, u32[]{:S(2)}) copy-start(bf16[128,4096]{1,0:T(8,128)(2,1)} %o_ref.1) | copy-start | bytes 3145732
  5.0 0.9 %copy-start.3 = (bf16[128,512]{1,0:T(8,128)(2,1)S(1)}, bf16[128,512]{1,0:T(8,128)(2,1)}, u32[]{:S(2)}) copy-start(bf16[128,512]{1,0:T(8,128)(2,1)} %k_ref.1) | copy-start | bytes 393220
  5.9 0.9 %copy-start.4 = (bf16[128,512]{1,0:T(8,128)(2,1)S(1)}, bf16[128,512]{1,0:T(8,128)(2,1)}, u32[]{:S(2)}) copy-start(bf16[128,512]{1,0:T(8,128)(2,1)} %v_ref.1) | copy-start | bytes 393220

commit v2 on v1

v2 whole, which is shorter than its diff:
```python
import functools
import math

import jax
import jax.numpy as jnp
from jax import lax
from jax.experimental import pallas as pl
from jax.experimental.pallas import tpu as pltpu
from jax.sharding import PartitionSpec as P

HEAD_DIM = 128
HEADS = 32
KV_HEADS = 4
BLOCKS = 9
EVENS = 5
PAIRS = 4
DOC_ROWS = 16
CHUNK = 3


def to(rank):
    return dict(device_id={"ctx": rank}, device_id_type=pl.DeviceIdType.MESH)


def kernel(
    ranks,
    q_ref,
    k_ref,
    v_ref,
    g_ref,
    o_ref,
    doc_ref,
    dq_ref,
    dk_ref,
    dv_ref,
    win,
    q_buf,
    g_buf,
    o_buf,
    doc_buf,
    scores,
    weights,
    lows,
    bias,
    acc_k,
    acc_v,
    sum_k,
    sum_v,
    sib_out,
    sib_in,
    x_out,
    x_in,
    z_out,
    z_in,
    in_send,
    in_recv,
    back_send,
    back_recv,
    kv_sem,
    row_sem,
):
    rows = q_buf.shape[0]
    span = BLOCKS * rows
    scale = 1.0 / math.sqrt(HEAD_DIM)
    exp_scale = scale * math.log2(math.e)
    rank = lax.axis_index("ctx")
    core = rank % 2
    col = (rank // 2) % 2
    sibling = rank + 1 - 2 * core
    partner = rank + 2 - 4 * col
    up4, down4, down8 = rank + 4 < ranks, rank >= 4, rank >= 8
    middle = up4 & down4

    barrier = pltpu.get_barrier_semaphore()
    for peer in (sibling, partner):
        pl.semaphore_signal(barrier, inc=1, **to(peer))
    for there, peer in ((up4, rank + 4), (down4, rank - 4)):

        @pl.when(there)
        def _(peer=peer):
            pl.semaphore_signal(barrier, inc=1, **to(peer))

    loads = [pltpu.make_async_copy(doc_ref, doc_buf, row_sem.at[3])]
    for g in range(KV_HEADS):
        cols = pl.ds(g * HEAD_DIM, HEAD_DIM)
        for n, src in ((0, k_ref), (1, v_ref)):
            dst = win.at[g, 0, pl.ds(n * rows, rows)]
            loads.append(pltpu.make_async_copy(src.at[:, cols], dst, kv_sem.at[g, n]))
    for n, (src, dst) in enumerate(((q_ref, q_buf), (g_ref, g_buf), (o_ref, o_buf))):
        loads.append(pltpu.make_async_copy(src, dst, row_sem.at[n]))
    for load in loads:
        load.start()

    for g in range(KV_HEADS):
        for slot, there in ((2, down4), (4, down8)):

            @pl.when(jnp.logical_not(there))
            def _(g=g, slot=slot):
                win[g, slot, 0 : 2 * rows, :] = jnp.zeros((2 * rows, HEAD_DIM), jnp.bfloat16)
                if g == 0:
                    win[g, slot, 2 * rows :, :] = jnp.full((DOC_ROWS, HEAD_DIM), -1.0, jnp.bfloat16)

    loads[0].wait()
    own_doc = doc_buf[...].astype(jnp.float32)
    win[0, 0, 2 * rows :, :] = jnp.broadcast_to(own_doc, (DOC_ROWS, rows)).astype(jnp.bfloat16)
    near = [there.astype(jnp.int32) for there in (up4, down4)]
    pl.semaphore_wait(barrier, 2 + sum(near))

    def part(g, slot):
        return win.at[g, slot, pl.ds(0, 2 * rows + (DOC_ROWS if g == 0 else 0))]

    def in_z(g, hop):
        return pltpu.make_async_remote_copy(
            src_ref=part(g, 2 * hop),
            dst_ref=part(g, 2 * hop + 2),
            send_sem=in_send.at[g, hop],
            recv_sem=in_recv.at[g, hop],
            **to(rank + 4),
        )

    def in_x(g, half):
        return pltpu.make_async_remote_copy(
            src_ref=part(g, 2 * col + 2 * half),
            dst_ref=part(g, 1 + 2 * half),
            send_sem=in_send.at[g, 2 + half],
            recv_sem=in_recv.at[g, 2 + half],
            **to(partner),
        )

    def in_sib(g):
        return pltpu.make_async_remote_copy(
            src_ref=part(g, pl.ds(core, 4)),
            dst_ref=part(g, pl.ds(EVENS, 4)),
            send_sem=in_send.at[g, 4],
            recv_sem=in_recv.at[g, 4],
            **to(sibling),
        )

    def send_own(g):
        loads[1 + 2 * g].wait()
        loads[2 + 2 * g].wait()

        @pl.when(up4)
        def _():
            in_z(g, 0).start()

        @pl.when(col == 0)
        def _():
            in_x(g, 0).start()

    def send_four(g):
        @pl.when(down4)
        def _():
            in_z(g, 0).wait_recv()

        @pl.when(middle)
        def _():
            in_z(g, 1).start()

        @pl.when(col == 0)
        def _():
            in_x(g, 1).start()

        @pl.when(col == 1)
        def _():
            in_x(g, 0).start()

    def send_eight(g):
        @pl.when(down8)
        def _():
            in_z(g, 1).wait_recv()

        @pl.when(col == 1)
        def _():
            in_x(g, 1).start()

    def send_sib(g):
        in_x(g, 0).wait_recv()
        in_x(g, 1).wait_recv()
        in_sib(g).start()

    def back_sib(g):
        return pltpu.make_async_remote_copy(
            src_ref=sib_out.at[g],
            dst_ref=sib_in.at[g],
            send_sem=back_send.at[g, 0],
            recv_sem=back_recv.at[g, 0],
            **to(sibling),
        )

    def back_x(g):
        return pltpu.make_async_remote_copy(
            src_ref=x_out.at[g],
            dst_ref=x_in.at[g],
            send_sem=back_send.at[g, 1],
            recv_sem=back_recv.at[g, 1],
            **to(partner),
        )

    def back_z(g, hop):
        return pltpu.make_async_remote_copy(
            src_ref=z_out.at[g, hop],
            dst_ref=z_in.at[g, hop],
            send_sem=back_send.at[g, 2 + hop],
            recv_sem=back_recv.at[g, 2 + hop],
            **to(rank - 4),
        )

    def stage_sib(g):
        for j in range(4):
            sib_out[g, j, 0:rows, :] = acc_k[EVENS + j].astype(jnp.bfloat16)
            sib_out[g, j, rows:, :] = acc_v[EVENS + j].astype(jnp.bfloat16)
        back_sib(g).start()
        sum_k[...] = acc_k[0:EVENS]
        sum_v[...] = acc_v[0:EVENS]

    def stage_x(g):
        back_sib(g).wait_recv()
        for j in range(4):
            sum_k[core + j] += sib_in[g, j, 0:rows, :].astype(jnp.float32)
            sum_v[core + j] += sib_in[g, j, rows:, :].astype(jnp.float32)
        for half in range(2):
            x_out[g, half, 0:rows, :] = sum_k[1 + 2 * half].astype(jnp.bfloat16)
            x_out[g, half, rows:, :] = sum_v[1 + 2 * half].astype(jnp.bfloat16)
        back_x(g).start()

    def stage_z(g):
        back_x(g).wait_recv()
        for half in range(2):
            slot = 2 * col + 2 * half
            sum_k[slot] += x_in[g, half, 0:rows, :].astype(jnp.float32)
            sum_v[slot] += x_in[g, half, rows:, :].astype(jnp.float32)

        @pl.when(down8)
        def _():
            z_out[g, 0, 0:rows, :] = sum_k[4].astype(jnp.bfloat16)
            z_out[g, 0, rows:, :] = sum_v[4].astype(jnp.bfloat16)
            back_z(g, 0).start()

    def stage_four(g):
        @pl.when(middle)
        def _():
            back_z(g, 0).wait_recv()
            sum_k[2] += z_in[g, 0, 0:rows, :].astype(jnp.float32)
            sum_v[2] += z_in[g, 0, rows:, :].astype(jnp.float32)

        @pl.when(down4)
        def _():
            z_out[g, 1, 0:rows, :] = sum_k[2].astype(jnp.bfloat16)
            z_out[g, 1, rows:, :] = sum_v[2].astype(jnp.bfloat16)
            back_z(g, 1).start()

    def finish(g):
        @pl.when(up4)
        def _():
            back_z(g, 1).wait_recv()
            sum_k[0] += z_in[g, 1, 0:rows, :].astype(jnp.float32)
            sum_v[0] += z_in[g, 1, rows:, :].astype(jnp.float32)

        cols = pl.ds(pl.multiple_of(g * HEAD_DIM, HEAD_DIM), HEAD_DIM)
        dk_ref[:, cols] = (sum_k[0] * scale).astype(jnp.bfloat16)
        dv_ref[:, cols] = sum_v[0].astype(jnp.bfloat16)

    send_own(0)
    send_four(0)
    send_own(1)
    send_eight(0)
    send_four(1)
    send_sib(0)
    send_own(2)
    for load in loads[-3:]:
        load.wait()
    in_sib(0).wait_recv()

    row_no = lax.broadcasted_iota(jnp.int32, (rows, rows), 0)
    col_no = lax.broadcasted_iota(jnp.int32, (rows, rows), 1)
    for slot in range(BLOCKS):
        line = win[0, slot, 2 * rows :, :].astype(jnp.float32)[0:1]
        key_doc = jnp.broadcast_to(line, (rows, rows)).T
        seen = key_doc == own_doc
        if slot == 0:
            seen = seen & (row_no <= col_no)
        bias[slot * rows : (slot + 1) * rows, :] = jnp.where(seen, 0.0, -1e30)

    def step(t, carry):
        g, pair = t // PAIRS, t % PAIRS

        def at(now, *todo):
            @pl.when(t == now)
            def _():
                for call, head in todo:
                    call(head)

        def wait_sib(head):
            in_sib(head).wait_recv()

        at(0, (send_eight, 1), (send_four, 2), (send_own, 3))
        at(1, (send_sib, 1))
        at(2, (send_eight, 2), (send_four, 3))
        at(3, (send_sib, 2))
        at(4, (wait_sib, 1), (send_eight, 3))
        at(5, (send_sib, 3))
        at(8, (wait_sib, 2))
        at(12, (wait_sib, 3))

        @pl.when(pair == 0)
        def _():
            acc_k[...] = jnp.zeros_like(acc_k)
            acc_v[...] = jnp.zeros_like(acc_v)

        first = pl.ds(pl.multiple_of(t * 2 * HEAD_DIM, HEAD_DIM), HEAD_DIM)
        second = pl.ds(pl.multiple_of(t * 2 * HEAD_DIM + HEAD_DIM, HEAD_DIM), HEAD_DIM)
        q = jnp.concatenate([q_buf[:, first], q_buf[:, second]], axis=0)
        grad = jnp.concatenate([g_buf[:, first], g_buf[:, second]], axis=0).astype(jnp.float32)
        out = jnp.concatenate([o_buf[:, first], o_buf[:, second]], axis=0).astype(jnp.float32)
        delta = jnp.sum((grad * out).T, axis=0, keepdims=True)
        nt = (((1,), (1,)), ((), ()))
        tn = (((0,), (0,)), ((), ()))
        top = None
        for c in range(0, BLOCKS, CHUNK):
            keys = win[g, c : c + CHUNK, 0:rows, :].reshape(CHUNK * rows, HEAD_DIM)
            mask = bias[c * rows : (c + CHUNK) * rows, :]
            piece = lax.dot_general(keys, q, nt, preferred_element_type=jnp.float32)
            piece = piece + jnp.concatenate([mask, mask], axis=1)
            scores[c * rows : (c + CHUNK) * rows, :] = piece
            high = jnp.max(piece.reshape(-1, 8, 2 * rows), axis=0)
            top = high if top is None else jnp.maximum(top, high)
        top = jnp.max(top, axis=0, keepdims=True)
        total = None
        for c in range(BLOCKS):
            piece = jnp.exp2((scores[c * rows : (c + 1) * rows, :] - top) * exp_scale)
            weights[c * rows : (c + 1) * rows, :] = piece.astype(jnp.bfloat16)
            more = jnp.sum(piece.reshape(-1, 8, 2 * rows), axis=0)
            total = more if total is None else total + more
        inverse = 1.0 / jnp.sum(total, axis=0, keepdims=True)
        delta = delta * inverse
        grad = (grad * jnp.broadcast_to(inverse, (HEAD_DIM, 2 * rows)).T).astype(jnp.bfloat16)
        for c in range(0, BLOCKS, CHUNK):
            vals = win[g, c : c + CHUNK, rows : 2 * rows, :].reshape(CHUNK * rows, HEAD_DIM)
            piece = lax.dot_general(vals, grad, nt, preferred_element_type=jnp.float32)
            held = weights[c * rows : (c + CHUNK) * rows, :].astype(jnp.float32)
            lows[c * rows : (c + CHUNK) * rows, :] = (held * (piece - delta)).astype(jnp.bfloat16)
        for c in range(0, BLOCKS, CHUNK):
            here = slice(c * rows, (c + CHUNK) * rows)
            acc_v[c : c + CHUNK] += jnp.dot(
                weights[here, :], grad, preferred_element_type=jnp.float32
            ).reshape(CHUNK, rows, HEAD_DIM)
            acc_k[c : c + CHUNK] += jnp.dot(
                lows[here, :], q, preferred_element_type=jnp.float32
            ).reshape(CHUNK, rows, HEAD_DIM)
        keys = win[g, :, 0:rows, :].reshape(span, HEAD_DIM)
        dq = lax.dot_general(lows[...], keys, tn, preferred_element_type=jnp.float32) * scale
        dq = dq.astype(jnp.bfloat16)
        dq_ref[:, first] = dq[0:rows]
        dq_ref[:, second] = dq[rows:]

        @pl.when((pair == 0) & (g > 0))
        def _():
            stage_x(g - 1)

        @pl.when((pair == 1) & (g > 0))
        def _():
            stage_z(g - 1)

        @pl.when((pair == 2) & (g > 0))
        def _():
            stage_four(g - 1)

        @pl.when((pair == 3) & (g > 0))
        def _():
            finish(g - 1)

        @pl.when(pair == 3)
        def _():
            stage_sib(g)

        return carry

    lax.fori_loop(0, KV_HEADS * PAIRS, step, 0)
    last = KV_HEADS - 1
    stage_x(last)
    stage_z(last)
    stage_four(last)
    finish(last)
    for g in range(KV_HEADS):
        in_x(g, 0).wait_send()
        in_x(g, 1).wait_send()
        in_sib(g).wait_send()
        back_sib(g).wait_send()
        back_x(g).wait_send()
        for hop, there_in, there_out in ((0, up4, down8), (1, middle, down4)):

            @pl.when(there_in)
            def _(g=g, hop=hop):
                in_z(g, hop).wait_send()

            @pl.when(there_out)
            def _(g=g, hop=hop):
                back_z(g, hop).wait_send()


def on_device(queries, keys, values, out_grad, attn_out, doc_ids):
    ranks = lax.axis_size("ctx")
    rows = queries.shape[0]
    bf16, f32 = jnp.bfloat16, jnp.float32
    vmem = pl.BlockSpec(memory_space=pltpu.VMEM)
    block = (rows, HEAD_DIM)
    pair = (2 * rows, HEAD_DIM)
    return pl.pallas_call(
        functools.partial(kernel, ranks),
        out_shape=(
            jax.ShapeDtypeStruct(queries.shape, bf16),
            jax.ShapeDtypeStruct(keys.shape, bf16),
            jax.ShapeDtypeStruct(values.shape, bf16),
        ),
        in_specs=[pl.BlockSpec(memory_space=pl.ANY)] * 6,
        out_specs=(vmem,) * 3,
        scratch_shapes=[
            pltpu.VMEM((KV_HEADS, BLOCKS, 2 * rows + DOC_ROWS, HEAD_DIM), bf16),
            pltpu.VMEM(queries.shape, bf16),
            pltpu.VMEM(queries.shape, bf16),
            pltpu.VMEM(queries.shape, bf16),
            pltpu.VMEM((1, rows), jnp.int32),
            pltpu.VMEM((BLOCKS * rows, 2 * rows), f32),
            pltpu.VMEM((BLOCKS * rows, 2 * rows), bf16),
            pltpu.VMEM((BLOCKS * rows, 2 * rows), bf16),
            pltpu.VMEM((BLOCKS * rows, rows), f32),
            pltpu.VMEM((BLOCKS,) + block, f32),
            pltpu.VMEM((BLOCKS,) + block, f32),
            pltpu.VMEM((EVENS,) + block, f32),
            pltpu.VMEM((EVENS,) + block, f32),
            pltpu.VMEM((KV_HEADS, 4) + pair, bf16),
            pltpu.VMEM((KV_HEADS, 4) + pair, bf16),
            pltpu.VMEM((KV_HEADS, 2) + pair, bf16),
            pltpu.VMEM((KV_HEADS, 2) + pair, bf16),
            pltpu.VMEM((KV_HEADS, 2) + pair, bf16),
            pltpu.VMEM((KV_HEADS, 2) + pair, bf16),
            pltpu.SemaphoreType.DMA((KV_HEADS, 5)),
            pltpu.SemaphoreType.DMA((KV_HEADS, 5)),
            pltpu.SemaphoreType.DMA((KV_HEADS, 4)),
            pltpu.SemaphoreType.DMA((KV_HEADS, 4)),
            pltpu.SemaphoreType.DMA((KV_HEADS, 2)),
            pltpu.SemaphoreType.DMA((4,)),
        ],
        compiler_params=pltpu.CompilerParams(
            collective_id=0, has_side_effects=True, vmem_limit_bytes=48 * 1024 * 1024
        ),
    )(queries, keys, values, out_grad, attn_out, doc_ids.reshape(1, rows))


def solution(mesh):
    spec = P(("groups", "ctx"), None)
    return jax.shard_map(
        on_device,
        mesh=mesh,
        in_specs=(spec,) * 5 + (P(("groups", "ctx")),),
        out_specs=(spec,) * 3,
        check_vma=False,
    )
```

time: 81.2 us -> 77.8 us (0.958)
  Pallas kernels: 71.8 us -> 68.5 us
    pallas_call x1, Pallas kernels: 71.8 us -> 68.5 us  [on_device(): pl.pallas_call(functools.partial(kernel, ranks), out_shape=(jax.ShapeDtyp...]
where the time goes in v2:
time: 77.8 us; the launch traced here: 77.5 us
  Pallas kernels  68.5 us (88%)
  local copies, waits for them, and re-layouts  8.41 us (11%)
    pallas_call x1, Pallas kernels, on_device(): pl.pallas_call(functools.partial(kernel, ranks), out_shape=(jax.ShapeDtyp...  68.5 us
    unnamed x15, local copies, waits for them, and re-layouts  8.41 us

profile of v2, /device:TPU:0, one launch (start us, length us, event | category | flops | bytes accessed | tf_op | source)
XLA Modules:
  0.0 77.5 jit_solution(16126066466349597514)
XLA Ops:
  0.6 0.0 copy-start.5
  0.6 0.6 copy-done.5
  1.3 0.0 copy-start
  1.3 1.2 %copy-done = bf16[128,4096]{1,0:T(8,128)(2,1)S(1)} copy-done((bf16[128,4096]{1,0:T(8,128)(2,1)S(1)}, bf16[128,4096]{1,0:T(8,128)(2,1)}, u32[]{:S(2)}) %copy-start) | copy-done | bytes 1048600
  2.5 0.0 copy-start.1
  2.5 1.2 %copy-done.1 = bf16[128,4096]{1,0:T(8,128)(2,1)S(1)} copy-done((bf16[128,4096]{1,0:T(8,128)(2,1)S(1)}, bf16[128,4096]{1,0:T(8,128)(2,1)}, u32[]{:S(2)}) %copy-start.1) | copy-done | bytes 1048600
  3.7 0.0 copy-start.2
  3.7 1.2 %copy-done.2 = bf16[128,4096]{1,0:T(8,128)(2,1)S(1)} copy-done((bf16[128,4096]{1,0:T(8,128)(2,1)S(1)}, bf16[128,4096]{1,0:T(8,128)(2,1)}, u32[]{:S(2)}) %copy-start.2) | copy-done | bytes 1048600
  5.0 0.0 copy-start.3
  5.0 0.9 %copy-done.3 = bf16[128,512]{1,0:T(8,128)(2,1)S(1)} copy-done((bf16[128,512]{1,0:T(8,128)(2,1)S(1)}, bf16[128,512]{1,0:T(8,128)(2,1)}, u32[]{:S(2)}) %copy-start.3) | copy-done | bytes 131096
  5.9 0.0 copy-start.4
  5.9 0.9 %copy-done.4 = bf16[128,512]{1,0:T(8,128)(2,1)S(1)} copy-done((bf16[128,512]{1,0:T(8,128)(2,1)S(1)}, bf16[128,512]{1,0:T(8,128)(2,1)}, u32[]{:S(2)}) %copy-start.4) | copy-done | bytes 131096
  6.8 68.5 %shard_map.85 = (bf16[128,4096]{1,0:T(8,128)(2,1)S(1)}, bf16[128,512]{1,0:T(8,128)(2,1)S(1)}, bf16[128,512]{1,0:T(8,128)(2,1)S(1)}) custom-call(bf16[128,4096]{1,0:T(8,128)(2,1)S(1)} %copy-done, bf16[128,512]{1,0:T(8,128)(2,1)S(1)} %copy-done.3, bf16[128,512]{1,0:T(8,128)(2,1)S(1)} %copy-done.4, bf16[128,4096]{1,0:T(8,128)(2,1)S(1)} %copy-done.1, ...), custom_call_target="tpu_custom_call" | custom-call | tf_op jit(solution)/shard_map/pallas_call | solution.py:409
  75.2 1.0 %copy.12 = bf16[128,4096]{1,0:T(8,128)(2,1)} copy(bf16[128,4096]{1,0:T(8,128)(2,1)S(1)} %get-tuple-element.6) | data formatting | bytes 2097152
  76.2 0.7 copy.13
  76.9 0.7 copy.14
Async XLA Ops:
  0.6 0.7 copy-start.5
  1.3 1.2 %copy-start = (bf16[128,4096]{1,0:T(8,128)(2,1)S(1)}, bf16[128,4096]{1,0:T(8,128)(2,1)}, u32[]{:S(2)}) copy-start(bf16[128,4096]{1,0:T(8,128)(2,1)} %q_ref.1) | copy-start | bytes 3145732
  2.5 1.2 %copy-start.1 = (bf16[128,4096]{1,0:T(8,128)(2,1)S(1)}, bf16[128,4096]{1,0:T(8,128)(2,1)}, u32[]{:S(2)}) copy-start(bf16[128,4096]{1,0:T(8,128)(2,1)} %g_ref.1) | copy-start | bytes 3145732
  3.7 1.2 %copy-start.2 = (bf16[128,4096]{1,0:T(8,128)(2,1)S(1)}, bf16[128,4096]{1,0:T(8,128)(2,1)}, u32[]{:S(2)}) copy-start(bf16[128,4096]{1,0:T(8,128)(2,1)} %o_ref.1) | copy-start | bytes 3145732
  5.0 0.9 %copy-start.3 = (bf16[128,512]{1,0:T(8,128)(2,1)S(1)}, bf16[128,512]{1,0:T(8,128)(2,1)}, u32[]{:S(2)}) copy-start(bf16[128,512]{1,0:T(8,128)(2,1)} %k_ref.1) | copy-start | bytes 393220
  5.9 0.9 %copy-start.4 = (bf16[128,512]{1,0:T(8,128)(2,1)S(1)}, bf16[128,512]{1,0:T(8,128)(2,1)}, u32[]{:S(2)}) copy-start(bf16[128,512]{1,0:T(8,128)(2,1)} %v_ref.1) | copy-start | bytes 393220

commit v3 on v2

--- a/solution.py
+++ b/solution.py
@@ -211,55 +211,55 @@
             sib_out[g, j, 0:rows, :] = acc_k[EVENS + j].astype(jnp.bfloat16)
             sib_out[g, j, rows:, :] = acc_v[EVENS + j].astype(jnp.bfloat16)
         back_sib(g).start()
-        sum_k[...] = acc_k[0:EVENS]
-        sum_v[...] = acc_v[0:EVENS]
+        sum_k[g % 2] = acc_k[0:EVENS]
+        sum_v[g % 2] = acc_v[0:EVENS]
 
     def stage_x(g):
         back_sib(g).wait_recv()
         for j in range(4):
-            sum_k[core + j] += sib_in[g, j, 0:rows, :].astype(jnp.float32)
-            sum_v[core + j] += sib_in[g, j, rows:, :].astype(jnp.float32)
+            sum_k[g % 2, core + j] += sib_in[g, j, 0:rows, :].astype(jnp.float32)
+            sum_v[g % 2, core + j] += sib_in[g, j, rows:, :].astype(jnp.float32)
         for half in range(2):
-            x_out[g, half, 0:rows, :] = sum_k[1 + 2 * half].astype(jnp.bfloat16)
-            x_out[g, half, rows:, :] = sum_v[1 + 2 * half].astype(jnp.bfloat16)
+            x_out[g, half, 0:rows, :] = sum_k[g % 2, 1 + 2 * half].astype(jnp.bfloat16)
+            x_out[g, half, rows:, :] = sum_v[g % 2, 1 + 2 * half].astype(jnp.bfloat16)
         back_x(g).start()
 
     def stage_z(g):
         back_x(g).wait_recv()
         for half in range(2):
             slot = 2 * col + 2 * half
-            sum_k[slot] += x_in[g, half, 0:rows, :].astype(jnp.float32)
-            sum_v[slot] += x_in[g, half, rows:, :].astype(jnp.float32)
+            sum_k[g % 2, slot] += x_in[g, half, 0:rows, :].astype(jnp.float32)
+            sum_v[g % 2, slot] += x_in[g, half, rows:, :].astype(jnp.float32)
 
         @pl.when(down8)
         def _():
-            z_out[g, 0, 0:rows, :] = sum_k[4].astype(jnp.bfloat16)
-            z_out[g, 0, rows:, :] = sum_v[4].astype(jnp.bfloat16)
+            z_out[g, 0, 0:rows, :] = sum_k[g % 2, 4].astype(jnp.bfloat16)
+            z_out[g, 0, rows:, :] = sum_v[g % 2, 4].astype(jnp.bfloat16)
             back_z(g, 0).start()
 
     def stage_four(g):
         @pl.when(middle)
         def _():
             back_z(g, 0).wait_recv()
-            sum_k[2] += z_in[g, 0, 0:rows, :].astype(jnp.float32)
-            sum_v[2] += z_in[g, 0, rows:, :].astype(jnp.float32)
+            sum_k[g % 2, 2] += z_in[g, 0, 0:rows, :].astype(jnp.float32)
+            sum_v[g % 2, 2] += z_in[g, 0, rows:, :].astype(jnp.float32)
 
         @pl.when(down4)
         def _():
-            z_out[g, 1, 0:rows, :] = sum_k[2].astype(jnp.bfloat16)
-            z_out[g, 1, rows:, :] = sum_v[2].astype(jnp.bfloat16)
+            z_out[g, 1, 0:rows, :] = sum_k[g % 2, 2].astype(jnp.bfloat16)
+            z_out[g, 1, rows:, :] = sum_v[g % 2, 2].astype(jnp.bfloat16)
             back_z(g, 1).start()
 
     def finish(g):
         @pl.when(up4)
         def _():
             back_z(g, 1).wait_recv()
-            sum_k[0] += z_in[g, 1, 0:rows, :].astype(jnp.float32)
-            sum_v[0] += z_in[g, 1, rows:, :].astype(jnp.float32)
+            sum_k[g % 2, 0] += z_in[g, 1, 0:rows, :].astype(jnp.float32)
+            sum_v[g % 2, 0] += z_in[g, 1, rows:, :].astype(jnp.float32)
 
         cols = pl.ds(pl.multiple_of(g * HEAD_DIM, HEAD_DIM), HEAD_DIM)
-        dk_ref[:, cols] = (sum_k[0] * scale).astype(jnp.bfloat16)
-        dv_ref[:, cols] = sum_v[0].astype(jnp.bfloat16)
+        dk_ref[:, cols] = (sum_k[g % 2, 0] * scale).astype(jnp.bfloat16)
+        dv_ref[:, cols] = sum_v[g % 2, 0].astype(jnp.bfloat16)
 
     send_own(0)
     send_four(0)
@@ -354,21 +354,13 @@
         dq_ref[:, first] = dq[0:rows]
         dq_ref[:, second] = dq[rows:]
 
-        @pl.when((pair == 0) & (g > 0))
-        def _():
-            stage_x(g - 1)
-
-        @pl.when((pair == 1) & (g > 0))
-        def _():
-            stage_z(g - 1)
-
-        @pl.when((pair == 2) & (g > 0))
-        def _():
-            stage_four(g - 1)
-
-        @pl.when((pair == 3) & (g > 0))
-        def _():
-            finish(g - 1)
+        at(5, (stage_x, 0))
+        at(8, (stage_z, 0))
+        at(9, (stage_x, 1), (stage_four, 0))
+        at(11, (finish, 0))
+        at(12, (stage_z, 1))
+        at(13, (stage_x, 2), (stage_four, 1))
+        at(15, (finish, 1), (stage_z, 2))
 
         @pl.when(pair == 3)
         def _():
@@ -379,7 +371,9 @@
     lax.fori_loop(0, KV_HEADS * PAIRS, step, 0)
     last = KV_HEADS - 1
     stage_x(last)
+    stage_four(last - 1)
     stage_z(last)
+    finish(last - 1)
     stage_four(last)
     finish(last)
     for g in range(KV_HEADS):
@@ -427,8 +421,8 @@
             pltpu.VMEM((BLOCKS * rows, rows), f32),
             pltpu.VMEM((BLOCKS,) + block, f32),
             pltpu.VMEM((BLOCKS,) + block, f32),
-            pltpu.VMEM((EVENS,) + block, f32),
-            pltpu.VMEM((EVENS,) + block, f32),
+            pltpu.VMEM((2, EVENS) + block, f32),
+            pltpu.VMEM((2, EVENS) + block, f32),
             pltpu.VMEM((KV_HEADS, 4) + pair, bf16),
             pltpu.VMEM((KV_HEADS, 4) + pair, bf16),
             pltpu.VMEM((KV_HEADS, 2) + pair, bf16),

time: 77.8 us -> 69.1 us (0.89)
  Pallas kernels: 68.5 us -> 59.8 us
    pallas_call x1, Pallas kernels: 68.5 us -> 59.8 us  [on_device(): pl.pallas_call(functools.partial(kernel, ranks), out_shape=(jax.ShapeDtyp...]
where the time goes in v3:
time: 69.1 us; the launch traced here: 68.8 us
  Pallas kernels  59.8 us (87%)
  local copies, waits for them, and re-layouts  8.41 us (12%)
    pallas_call x1, Pallas kernels, on_device(): pl.pallas_call(functools.partial(kernel, ranks), out_shape=(jax.ShapeDtyp...  59.8 us
    unnamed x15, local copies, waits for them, and re-layouts  8.41 us

profile of v3, /device:TPU:0, one launch (start us, length us, event | category | flops | bytes accessed | tf_op | source)
XLA Modules:
  0.0 68.8 jit_solution(14976990504054653934)
XLA Ops:
  0.6 0.0 copy-start.5
  0.6 0.6 copy-done.5
  1.3 0.0 copy-start
  1.3 1.2 %copy-done = bf16[128,4096]{1,0:T(8,128)(2,1)S(1)} copy-done((bf16[128,4096]{1,0:T(8,128)(2,1)S(1)}, bf16[128,4096]{1,0:T(8,128)(2,1)}, u32[]{:S(2)}) %copy-start) | copy-done | bytes 1048600
  2.5 0.0 copy-start.1
  2.5 1.2 %copy-done.1 = bf16[128,4096]{1,0:T(8,128)(2,1)S(1)} copy-done((bf16[128,4096]{1,0:T(8,128)(2,1)S(1)}, bf16[128,4096]{1,0:T(8,128)(2,1)}, u32[]{:S(2)}) %copy-start.1) | copy-done | bytes 1048600
  3.7 0.0 copy-start.2
  3.7 1.2 %copy-done.2 = bf16[128,4096]{1,0:T(8,128)(2,1)S(1)} copy-done((bf16[128,4096]{1,0:T(8,128)(2,1)S(1)}, bf16[128,4096]{1,0:T(8,128)(2,1)}, u32[]{:S(2)}) %copy-start.2) | copy-done | bytes 1048600
  5.0 0.0 copy-start.3
  5.0 0.9 %copy-done.3 = bf16[128,512]{1,0:T(8,128)(2,1)S(1)} copy-done((bf16[128,512]{1,0:T(8,128)(2,1)S(1)}, bf16[128,512]{1,0:T(8,128)(2,1)}, u32[]{:S(2)}) %copy-start.3) | copy-done | bytes 131096
  5.9 0.0 copy-start.4
  5.9 0.9 %copy-done.4 = bf16[128,512]{1,0:T(8,128)(2,1)S(1)} copy-done((bf16[128,512]{1,0:T(8,128)(2,1)S(1)}, bf16[128,512]{1,0:T(8,128)(2,1)}, u32[]{:S(2)}) %copy-start.4) | copy-done | bytes 131096
  6.8 59.8 %shard_map.85 = (bf16[128,4096]{1,0:T(8,128)(2,1)S(1)}, bf16[128,512]{1,0:T(8,128)(2,1)S(1)}, bf16[128,512]{1,0:T(8,128)(2,1)S(1)}) custom-call(bf16[128,4096]{1,0:T(8,128)(2,1)S(1)} %copy-done, bf16[128,512]{1,0:T(8,128)(2,1)S(1)} %copy-done.3, bf16[128,512]{1,0:T(8,128)(2,1)S(1)} %copy-done.4, bf16[128,4096]{1,0:T(8,128)(2,1)S(1)} %copy-done.1, ...), custom_call_target="tpu_custom_call" | custom-call | tf_op jit(solution)/shard_map/pallas_call | solution.py:403
  66.5 1.0 %copy.12 = bf16[128,4096]{1,0:T(8,128)(2,1)} copy(bf16[128,4096]{1,0:T(8,128)(2,1)S(1)} %get-tuple-element.6) | data formatting | bytes 2097152
  67.5 0.7 copy.13
  68.2 0.7 copy.14
Async XLA Ops:
  0.6 0.7 copy-start.5
  1.3 1.2 %copy-start = (bf16[128,4096]{1,0:T(8,128)(2,1)S(1)}, bf16[128,4096]{1,0:T(8,128)(2,1)}, u32[]{:S(2)}) copy-start(bf16[128,4096]{1,0:T(8,128)(2,1)} %q_ref.1) | copy-start | bytes 3145732
  2.5 1.2 %copy-start.1 = (bf16[128,4096]{1,0:T(8,128)(2,1)S(1)}, bf16[128,4096]{1,0:T(8,128)(2,1)}, u32[]{:S(2)}) copy-start(bf16[128,4096]{1,0:T(8,128)(2,1)} %g_ref.1) | copy-start | bytes 3145732
  3.7 1.2 %copy-start.2 = (bf16[128,4096]{1,0:T(8,128)(2,1)S(1)}, bf16[128,4096]{1,0:T(8,128)(2,1)}, u32[]{:S(2)}) copy-start(bf16[128,4096]{1,0:T(8,128)(2,1)} %o_ref.1) | copy-start | bytes 3145732
  5.0 0.9 %copy-start.3 = (bf16[128,512]{1,0:T(8,128)(2,1)S(1)}, bf16[128,512]{1,0:T(8,128)(2,1)}, u32[]{:S(2)}) copy-start(bf16[128,512]{1,0:T(8,128)(2,1)} %k_ref.1) | copy-start | bytes 393220
  5.9 0.9 %copy-start.4 = (bf16[128,512]{1,0:T(8,128)(2,1)S(1)}, bf16[128,512]{1,0:T(8,128)(2,1)}, u32[]{:S(2)}) copy-start(bf16[128,512]{1,0:T(8,128)(2,1)} %v_ref.1) | copy-start | bytes 393220

commit v4 on v3

--- a/solution.py
+++ b/solution.py
@@ -127,12 +127,12 @@
             **to(partner),
         )
 
-    def in_sib(g):
-        return pltpu.make_async_remote_copy(
-            src_ref=part(g, pl.ds(core, 4)),
-            dst_ref=part(g, pl.ds(EVENS, 4)),
-            send_sem=in_send.at[g, 4],
-            recv_sem=in_recv.at[g, 4],
+    def in_sib(g, half):
+        return pltpu.make_async_remote_copy(
+            src_ref=part(g, pl.ds(core + 2 * half, 2)),
+            dst_ref=part(g, pl.ds(EVENS + 2 * half, 2)),
+            send_sem=in_send.at[g, 4 + half],
+            recv_sem=in_recv.at[g, 4 + half],
             **to(sibling),
         )
 
@@ -176,8 +176,9 @@
 
     def send_sib(g):
         in_x(g, 0).wait_recv()
+        in_sib(g, 0).start()
         in_x(g, 1).wait_recv()
-        in_sib(g).start()
+        in_sib(g, 1).start()
 
     def back_sib(g):
         return pltpu.make_async_remote_copy(
@@ -270,7 +271,8 @@
     send_own(2)
     for load in loads[-3:]:
         load.wait()
-    in_sib(0).wait_recv()
+    in_sib(0, 0).wait_recv()
+    in_sib(0, 1).wait_recv()
 
     row_no = lax.broadcasted_iota(jnp.int32, (rows, rows), 0)
     col_no = lax.broadcasted_iota(jnp.int32, (rows, rows), 1)
@@ -292,7 +294,8 @@
                     call(head)
 
         def wait_sib(head):
-            in_sib(head).wait_recv()
+            in_sib(head, 0).wait_recv()
+            in_sib(head, 1).wait_recv()
 
         at(0, (send_eight, 1), (send_four, 2), (send_own, 3))
         at(1, (send_sib, 1))
@@ -360,12 +363,13 @@
         at(11, (finish, 0))
         at(12, (stage_z, 1))
         at(13, (stage_x, 2), (stage_four, 1))
-        at(15, (finish, 1), (stage_z, 2))
+        at(15, (finish, 1))
 
         @pl.when(pair == 3)
         def _():
             stage_sib(g)
 
+        at(15, (stage_z, 2))
         return carry
 
     lax.fori_loop(0, KV_HEADS * PAIRS, step, 0)
@@ -379,7 +383,8 @@
     for g in range(KV_HEADS):
         in_x(g, 0).wait_send()
         in_x(g, 1).wait_send()
-        in_sib(g).wait_send()
+        in_sib(g, 0).wait_send()
+        in_sib(g, 1).wait_send()
         back_sib(g).wait_send()
         back_x(g).wait_send()
         for hop, there_in, there_out in ((0, up4, down8), (1, middle, down4)):
@@ -407,7 +412,7 @@
             jax.ShapeDtypeStruct(keys.shape, bf16),
             jax.ShapeDtypeStruct(values.shape, bf16),
         ),
-        in_specs=[pl.BlockSpec(memory_space=pl.ANY)] * 6,
+        in_specs=[pl.BlockSpec(memory_space=pltpu.HBM)] * 6,
         out_specs=(vmem,) * 3,
         scratch_shapes=[
             pltpu.VMEM((KV_HEADS, BLOCKS, 2 * rows + DOC_ROWS, HEAD_DIM), bf16),
@@ -429,15 +434,15 @@
             pltpu.VMEM((KV_HEADS, 2) + pair, bf16),
             pltpu.VMEM((KV_HEADS, 2) + pair, bf16),
             pltpu.VMEM((KV_HEADS, 2) + pair, bf16),
-            pltpu.SemaphoreType.DMA((KV_HEADS, 5)),
-            pltpu.SemaphoreType.DMA((KV_HEADS, 5)),
+            pltpu.SemaphoreType.DMA((KV_HEADS, 6)),
+            pltpu.SemaphoreType.DMA((KV_HEADS, 6)),
             pltpu.SemaphoreType.DMA((KV_HEADS, 4)),
             pltpu.SemaphoreType.DMA((KV_HEADS, 4)),
             pltpu.SemaphoreType.DMA((KV_HEADS, 2)),
             pltpu.SemaphoreType.DMA((4,)),
         ],
         compiler_params=pltpu.CompilerParams(
-            collective_id=0, has_side_effects=True, vmem_limit_bytes=48 * 1024 * 1024
+            collective_id=0, has_side_effects=True, vmem_limit_bytes=60 * 1024 * 1024
         ),
     )(queries, keys, values, out_grad, attn_out, doc_ids.reshape(1, rows))
 

time: 69.1 us -> 65.2 us (0.944)
  local copies, waits for them, and re-layouts: 8.41 us -> 3.93 us
  Pallas kernels: 59.8 us -> 60.5 us
    unnamed x15 -> x7, local copies, waits for them, and re-layouts: 8.41 us -> 3.93 us
    pallas_call x1, Pallas kernels: 59.8 us -> 60.5 us  [on_device(): pl.pallas_call(functools.partial(kernel, ranks), out_shape=(jax.ShapeDtyp...]
where the time goes in v4:
time: 65.2 us; the launch traced here: 65 us
  Pallas kernels  60.5 us (93%)
  local copies, waits for them, and re-layouts  3.93 us (6%)
    pallas_call x1, Pallas kernels, on_device(): pl.pallas_call(functools.partial(kernel, ranks), out_shape=(jax.ShapeDtyp...  60.5 us
    unnamed x7, local copies, waits for them, and re-layouts  3.93 us

profile of v4, /device:TPU:0, one launch (start us, length us, event | category | flops | bytes accessed | tf_op | source)
XLA Modules:
  0.0 65.0 jit_solution(13795710752052217371)
XLA Ops:
  0.6 60.5 %shard_map.85 = (bf16[128,4096]{1,0:T(8,128)(2,1)}, bf16[128,512]{1,0:T(8,128)(2,1)}, bf16[128,512]{1,0:T(8,128)(2,1)}) custom-call(bf16[128,4096]{1,0:T(8,128)(2,1)} %q_ref.1, bf16[128,512]{1,0:T(8,128)(2,1)} %k_ref.1, bf16[128,512]{1,0:T(8,128)(2,1)} %v_ref.1, bf16[128,4096]{1,0:T(8,128)(2,1)} %g_ref.1, bf16[128,4096]{1,0:T(8,128)(2,1)} %o_ref.1, ...), custom_call_target="tpu_custom_call" | custom-call | tf_op jit(solution)/shard_map/pallas_call | solution.py:408
  61.1 0.0 copy-start.1
  61.1 2.3 %copy.12 = bf16[128,4096]{1,0:T(8,128)(2,1)} copy(bf16[128,4096]{1,0:T(8,128)(2,1)} %get-tuple-element.6) | data formatting | bytes 2097152
  63.4 0.0 copy-done.1
  63.4 0.0 copy-start
  63.4 0.7 %copy.13 = bf16[128,512]{1,0:T(8,128)(2,1)} copy(bf16[128,512]{1,0:T(8,128)(2,1)S(1)} %copy-done.1) | data formatting | bytes 262144
  64.1 0.3 copy-done
  64.4 0.7 %copy.14 = bf16[128,512]{1,0:T(8,128)(2,1)} copy(bf16[128,512]{1,0:T(8,128)(2,1)S(1)} %copy-done) | data formatting | bytes 262144
Async XLA Ops:
  61.1 2.3 %copy-start.1 = (bf16[128,512]{1,0:T(8,128)(2,1)S(1)}, bf16[128,512]{1,0:T(8,128)(2,1)}, u32[]{:S(2)}) copy-start(bf16[128,512]{1,0:T(8,128)(2,1)} %get-tuple-element.7) | copy-start | bytes 393220
  63.4 1.0 %copy-start = (bf16[128,512]{1,0:T(8,128)(2,1)S(1)}, bf16[128,512]{1,0:T(8,128)(2,1)}, u32[]{:S(2)}) copy-start(bf16[128,512]{1,0:T(8,128)(2,1)} %get-tuple-element.8) | copy-start | bytes 393220
